TPU v7x, 32 devices: a whole 2x2x4 slice. The times are simulated.
32 devices in a mesh: grp: 2 (over x), blk: 16 (over z, y, core).
Axes of the slice: x: 2, y: 2, z: 4, core: 2. Of those that a mesh axis runs over, the one named last changes fastest.
Arguments:
- left_values: bfloat16 [4096, 128], P(('grp', 'blk')), parts along dimension 0, may hold values from -6 to 6
- left_dirs: bfloat16 [4096, 128], P(('grp', 'blk')), parts along dimension 0, may hold values from -6 to 6
- left_pos: int32 [4096], P(('grp', 'blk')), parts along dimension 0, may hold values from 0 to 2047, each once
- right_dirs: bfloat16 [4096, 128], P(('grp', 'blk')), parts along dimension 0, may hold values from -0.5 to 0.5
- right_values: bfloat16 [4096, 128], P(('grp', 'blk')), parts along dimension 0, may hold values from -0.5 to 0.5
- right_pos: int32 [4096], P(('grp', 'blk')), parts along dimension 0, may hold values from 0 to 2047, each once
- sketch_seed: int32 [2], P('grp'), parts along dimension 0, may hold values from 0 to 1073741823
Outputs:
- sketch_loewner: float32 [4, 2048, 512], P('grp', 'blk'), parts along dimension 0
- sketch_shifted: float32 [4, 2048, 512], P('grp', 'blk'), parts along dimension 0
- gram_loewner: float32 [1024, 512], P('grp'), parts along dimension 0
- gram_shifted: float32 [1024, 512], P('grp'), parts along dimension 0
There are 2 independent parts, one for each index of `grp`. A program takes and returns all parts, laid end to end along the dimension named above; each array names one. Nothing has to cross between parts.
Inputs may be any that keep to these rules, and one draw needn't show every extreme that they name: `left_pos`: each of 0 to 2047 appears exactly once. `right_pos`: each of 0 to 2047 appears exactly once.
All inputs are finite; a program needn't handle non-finite values.
Results may differ from a plain program's by a relative error of at most 0.003.
Values may be sent and summed in bfloat16 or wider, within the bound.
A program may use at most 64 MiB of HBM per device.

v0:
```python
import math

import jax
import jax.numpy as jnp
from jax import lax
from jax.sharding import PartitionSpec as P

SKETCH = 512


def sketch_block(seed_value, first_row, row_count, sketch_width):
    row_index = first_row + jnp.arange(row_count, dtype=jnp.int32)[:, None]
    col_index = jnp.arange(2 * sketch_width, dtype=jnp.int32)[None, :]
    hashed = seed_value * 374761393 + row_index * 668265263 + col_index * 1274126177
    hashed = hashed ^ hashed >> 15 & 131071
    hashed = hashed * 2146121005
    hashed = hashed ^ hashed >> 13 & 524287
    hashed = hashed * 1948299397
    hashed = hashed ^ hashed >> 16 & 65535
    level_code = hashed >> 8 & 255
    return ((level_code.astype(jnp.float32) - 127.5) / 128.0).astype(jnp.bfloat16)


def four_forms(matrix):
    half_width = matrix.shape[1] // 2
    real_part = matrix[:, :half_width]
    imag_part = matrix[:, half_width:]
    return jnp.concatenate(
        [
            jnp.concatenate([real_part, -imag_part], 1),
            jnp.concatenate([imag_part, real_part], 1),
            jnp.concatenate([real_part, imag_part], 1),
            jnp.concatenate([-imag_part, real_part], 1),
        ],
        0,
    )


def real_form(first_real, first_imag, second_real, second_imag):
    upper_row = jnp.concatenate([first_real + second_real, second_imag - first_imag], 1)
    lower_row = jnp.concatenate([first_imag + second_imag, first_real - second_real], 1)
    return (upper_row, lower_row)


def pencil_blocks(
    left_values,
    left_dirs,
    left_freq,
    left_hat,
    right_dirs,
    right_values,
    right_freq,
    right_hat,
    sketch_rows,
):
    row_count = left_values.shape[0]
    col_count = right_dirs.shape[0]
    sketch_width = sketch_rows.shape[1] // 2
    upper_terms = jnp.dot(
        left_values, four_forms(right_dirs).T, preferred_element_type=jnp.float32
    ).reshape(row_count, 4, col_count)
    lower_terms = jnp.dot(
        left_dirs, four_forms(right_values).T, preferred_element_type=jnp.float32
    ).reshape(row_count, 4, col_count)
    differ = left_freq[:, None] - right_freq[None, :]
    summed = left_freq[:, None] + right_freq[None, :]
    hat_left = left_hat[:, None]
    hat_right = right_hat[None, :]
    loewner_real = (upper_terms[:, 1] - lower_terms[:, 1]) / differ
    loewner_imag = (lower_terms[:, 0] - upper_terms[:, 0]) / differ
    mirror_real = (upper_terms[:, 3] - lower_terms[:, 3]) / summed
    mirror_imag = (lower_terms[:, 2] - upper_terms[:, 2]) / summed
    shifted_real = (hat_left * upper_terms[:, 0] - hat_right * lower_terms[:, 0]) / differ
    shifted_imag = (hat_left * upper_terms[:, 1] - hat_right * lower_terms[:, 1]) / differ
    flipped_real = (hat_left * upper_terms[:, 2] + hat_right * lower_terms[:, 2]) / summed
    flipped_imag = (hat_left * upper_terms[:, 3] + hat_right * lower_terms[:, 3]) / summed
    loewner_upper, loewner_lower = real_form(loewner_real, loewner_imag, mirror_real, mirror_imag)
    shifted_upper, shifted_lower = real_form(shifted_real, shifted_imag, flipped_real, flipped_imag)
    blocks = jnp.concatenate(
        [loewner_upper, loewner_lower, shifted_upper, shifted_lower], 0
    ).astype(jnp.bfloat16)
    stacked_sketch = jnp.concatenate(
        [sketch_rows[:, :sketch_width], sketch_rows[:, sketch_width:]], 0
    )
    return jnp.dot(blocks, stacked_sketch, preferred_element_type=jnp.float32)


def gram_term(rows_block):
    return lax.dot_general(
        rows_block,
        rows_block,
        (((0,), (0,)), ((), ())),
        precision=lax.Precision.HIGHEST,
        preferred_element_type=jnp.float32,
    )


def per_device(left_values, left_dirs, left_pos, right_dirs, right_values, right_pos, sketch_seed):
    row_count = left_pos.shape[0]
    total_left = row_count * lax.axis_size("blk")
    left_freq = (2 * left_pos - total_left).astype(jnp.float32) + 0.25
    left_hat = left_freq / total_left
    seed_value = sketch_seed[0]
    initial = jnp.zeros((4 * row_count, SKETCH), jnp.float32)

    def sketch_of(offset, step_rows):
        return sketch_block(seed_value, offset, step_rows, SKETCH)

    piece_dirs = lax.all_gather(right_dirs, "blk", axis=0, tiled=True)
    piece_values = lax.all_gather(right_values, "blk", axis=0, tiled=True)
    piece_pos = lax.all_gather(right_pos, "blk", axis=0, tiled=True)
    piece_rows = piece_pos.shape[0]
    step_rows = math.gcd(piece_rows, 512)

    def one_step(counter, partial_value):
        offset = counter * step_rows
        dirs_part = lax.dynamic_slice_in_dim(piece_dirs, offset, step_rows, 0)
        values_part = lax.dynamic_slice_in_dim(piece_values, offset, step_rows, 0)
        pos_part = lax.dynamic_slice_in_dim(piece_pos, offset, step_rows, 0)
        right_freq = (2 * pos_part + 1 - total_left).astype(jnp.float32) + 0.25
        right_hat = right_freq / total_left
        return partial_value + pencil_blocks(
            left_values,
            left_dirs,
            left_freq,
            left_hat,
            dirs_part,
            values_part,
            right_freq,
            right_hat,
            sketch_of(offset, step_rows),
        )

    stacked = lax.fori_loop(0, piece_rows // step_rows, one_step, initial)
    pencils = stacked.reshape(2, 2, row_count, SKETCH)
    halves = stacked.reshape(2, 2 * row_count, SKETCH)
    gram_loewner, gram_shifted = lax.psum((gram_term(halves[0]), gram_term(halves[1])), "blk")
    return (
        pencils[0],
        pencils[1],
        gram_loewner / (2 * total_left),
        gram_shifted / (2 * total_left),
    )


def solution(mesh):
    return jax.shard_map(
        per_device,
        mesh=mesh,
        in_specs=(
            P(("grp", "blk"), None),
            P(("grp", "blk"), None),
            P(("grp", "blk")),
            P(("grp", "blk"), None),
            P(("grp", "blk"), None),
            P(("grp", "blk")),
            P("grp"),
        ),
        out_specs=(P("grp", "blk", None), P("grp", "blk", None), P("grp", None), P("grp", None)),
        check_vma=False,
    )
```

profile of v0, /device:TPU:0, one launch (start us, length us, event | category | flops | bytes accessed | tf_op | source)
XLA Modules:
  0.0 211.1 jit_solution(8385986523764771315)
XLA Ops:
  7.2 24.8 %all_gather.9 = bf16[2048,128]{1,0:T(8,128)(2,1)S(1)} all-gather(bf16[128,128]{1,0:T(8,128)(2,1)} %param.12), channel_id=1, replica_groups=mesh['grp'=2,'blk'=16] {'blk'}, dimensions={0}, use_global_device_ids=true | all-gather | bytes 557056 | tf_op jit(solution)/shard_map/all_gather | solution.py:109
  32.0 19.1 %all_gather.10 = bf16[2048,128]{1,0:T(8,128)(2,1)S(1)} all-gather(bf16[128,128]{1,0:T(8,128)(2,1)} %param.13), channel_id=1, replica_groups=mesh['grp'=2,'blk'=16] {'blk'}, dimensions={0}, use_global_device_ids=true | all-gather | bytes 557056 | tf_op jit(solution)/shard_map/all_gather | solution.py:110
  51.2 18.7 %all-gather = s32[16,1,128]{2,1,0:T(1,128)S(1)} all-gather(s32[1,1,128]{2,1,0:T(1,128)S(1)} %bitcast.166), channel_id=1, replica_groups=mesh['grp'=2,'blk'=16] {'blk'}, dimensions={0}, use_global_device_ids=true | all-gather | bytes 8704 | tf_op jit(solution)/shard_map/all_gather | solution.py:111
  70.5 31.3 %while.18 = (s32[]{:T(128)}, f32[512,512]{1,0:T(8,128)S(1)}, bf16[2048,128]{1,0:T(8,128)(2,1)S(1)}, bf16[128,128]{1,0:T(8,128)(2,1)}, bf16[2048,128]{1,0:T(8,128...) while((s32[]{:T(128)}, f32[512,512]{1,0:T(8,128)S(1)}, ...), condition=%wide.region_1.0_spmd.clone, body=%wide.region_0.0_spmd.clone.sunk | while | flops 702616576 | bytes 16612081 | solution.py:134
  70.8 1.1 fusion.82
  71.9 1.1 fusion.83
  73.3 1.0 add_convert_fusion.7
  74.3 0.9 subtract_convert_fusion.5
  75.2 1.1 multiply_convert_fusion.2
  76.3 2.0 convolution_add_fusion.2
  78.6 1.1 fusion.82
  79.7 1.1 fusion.83
  81.1 1.0 add_convert_fusion.7
  82.1 0.9 subtract_convert_fusion.5
  83.0 1.1 multiply_convert_fusion.2
  84.1 2.0 convolution_add_fusion.2
  86.4 1.1 fusion.82
  87.5 1.1 fusion.83
  88.9 1.0 add_convert_fusion.7
  89.9 0.9 subtract_convert_fusion.5
  90.8 1.1 multiply_convert_fusion.2
  91.9 2.0 convolution_add_fusion.2
  94.2 1.1 fusion.82
  95.3 1.1 fusion.83
  96.7 1.0 add_convert_fusion.7
  98.6 1.1 multiply_convert_fusion.2
  99.8 2.0 convolution_add_fusion.2
  101.7 2.0 fusion.57
  103.8 2.0 fusion.55
  105.8 1.0 fusion.62
  106.8 94.3 %all-reduce.3.cloned.1.call-done = (f32[512,512]{1,0:T(8,128)}, f32[512,512]{1,0:T(8,128)}) async-done(((f32[512,512]{1,0:T(8,128)}, f32[512,512]{1,0:T(8,128)}), (f32[512,512]{1,0:T(8,128)}, f32[512,512]{1,0:T(8,128)})) %all-reduce.3.cloned.1.call-update) | async-done | bytes 2097168 | tf_op jit(solution)/shard_map/psum | solution.py:137
  201.2 3.1 %broadcast_multiply_fusion.1 = (f32[512,512]{1,0:T(8,128)}, f32[512,512]{1,0:T(8,128)}) fusion(f32[512,512]{1,0:T(8,128)} %get-tuple-element.377, f32[512,512]{1,0:T(8,128)} %get-tuple-element.376), kind=kLoop, calls=%fused_computation.91 | loop fusion | flops 524288 | bytes 4194304 | tf_op jit(solution)/shard_map/div | solution.py:142
  (37 shorter events, 3.5 us)
Async XLA Ops:
  7.2 44.0 %copy-start.1 = (s32[128]{0:T(128)S(1)}, s32[128]{0:T(128)}, u32[]{:S(2)}) copy-start(s32[128]{0:T(128)} %param.11) | copy-start | bytes 1540
  7.2 44.0 %copy-start = (s32[128]{0:T(128)S(1)}, s32[128]{0:T(128)}, u32[]{:S(2)}) copy-start(s32[128]{0:T(128)} %param.14) | copy-start | bytes 1540
  7.2 194.0 %all-reduce.3.cloned.1.call-start = ((), (), s32[]{:S(2)}) async-start(), calls=%async_computation | async-start | bytes 4194304 | tf_op jit(solution)/shard_map/psum | solution.py:137
Sparse Core Ops, SparseCore 0:
  105.9 95.1 all-reduce.2
where the time goes:
time: 212 us; the launch traced here: 211 us
  waiting for transfers between devices  94.3 us (44%)
  blocking collectives  62.6 us (30%)
  matrix products  20.7 us (10%)
  other arithmetic  17 us (8%)
  between operations  14.7 us (7%)
    psum x1, waiting for transfers between devices, per_device(): lax.psum((gram_term(halves[0]), gram_term(halves[1])), 'blk')  94.3 us
    all_gather x1, blocking collectives, per_device(): piece_dirs = lax.all_gather(right_dirs, 'blk', axis=0, tiled=True)  24.8 us
    all_gather x1, blocking collectives, per_device(): piece_values = lax.all_gather(right_values, 'blk', axis=0, tiled=True)  19.1 us
    all_gather x1, blocking collectives, per_device(): piece_pos = lax.all_gather(right_pos, 'blk', axis=0, tiled=True)  18.7 us
    another operation x12, other arithmetic  8.69 us
    dot_general x4, matrix products, pencil_blocks(): return jnp.dot(blocks, stacked_sketch, preferred_element_type=jnp.float32)  7.89 us
    dot_general x4, matrix products, pencil_blocks(): jnp.dot(left_dirs, four_forms(right_values).T, preferred_element_type=jnp...  4.37 us
    dot_general x4, matrix products, pencil_blocks(): jnp.dot(left_values, four_forms(right_dirs).T, preferred_element_type=jnp...  4.37 us
  transfers between devices with their start and end apart: 1, of which 1 were waited for; matrix products, arithmetic and copies ran while one was open for 0% of the time, Pallas kernels for 0%

commit v1 on v0

v1 whole, which is shorter than its diff:
```python
import functools

import jax
import jax.numpy as jnp
from jax import lax
from jax.experimental import pallas as pl
from jax.experimental.pallas import tpu as pltpu
from jax.sharding import PartitionSpec as P

SKETCH = 512
TILE = 128
TILES = [(p, q) for p in range(SKETCH // TILE) for q in range(p, SKETCH // TILE)]
HALF_STEP = (SKETCH * 1274126177 + 2**31) % 2**32 - 2**31
BF = jnp.bfloat16
F32 = jnp.float32


def chunk_rows_of(chips):
    per_chip = -(-len(TILES) * TILE // chips)
    return -(-per_chip // 16) * 16


def kernel(
    blk,
    lv_in, ld_in, lp_in, rd_in, rw_in, rp_in, seed,
    out, gall, mus,
    lv, ld, lp, lvp, ldp, lpp,
    gath, gpos,
    xs, fls, num, wblk, sk, acc, tacc, recv, trecv, tsend,
    zs, zrecv, gpart, yrecv, zsend, zgot,
    in_sem, pair_send, pair_recv, ring_send, ring_recv,
    pos_send, pos_recv, y_send, y_recv, z_send, z_recv,
    az_send, az_recv, ay_send, ay_recv, core_send, core_recv,
    mu_send, mu_recv,
):
    rows = lv_in.shape[0]
    chips = blk // 2
    half = chips // 2
    total = rows * blk
    me = lax.axis_index("blk")
    core = lax.rem(me, 2)
    chip = me // 2
    partner = me + 1 - 2 * core

    def device(chip_index):
        return {"blk": 2 * chip_index + core}

    row_y = lax.rem(chip, 2)
    row_z = chip // 2
    ring = (1 - 2 * row_y) * row_z + row_y * (2 * half - 1)

    def chip_at(position):
        q = lax.rem(position + 2 * chips, chips)
        y = q // half
        z = (1 - y) * q + y * (2 * half - 1 - q)
        return 2 * z + y

    own_slot = chips - 1
    ins = [
        pltpu.make_async_copy(src, dst, in_sem.at[i])
        for i, (src, dst) in enumerate((
            (rd_in, gath.at[own_slot, :, pl.ds(0, TILE)]),
            (rw_in, gath.at[own_slot, :, pl.ds(TILE, TILE)]),
            (rp_in, gpos.at[chip]),
            (lv_in, lv), (ld_in, ld), (lp_in, lp),
        ))
    ]
    for one in ins:
        one.start()

    barrier = pltpu.get_barrier_semaphore()
    pl.semaphore_signal(
        barrier, inc=1, device_id={"blk": partner}, device_id_type=pl.DeviceIdType.MESH
    )

    @pl.loop(1, chips)
    def _(o):
        pl.semaphore_signal(
            barrier, inc=1, device_id=device(lax.rem(chip + o, chips)),
            device_id_type=pl.DeviceIdType.MESH,
        )

    hr, hc = 16, 512
    base = (
        lax.broadcasted_iota(jnp.int32, (hr, hc), 0) * 668265263
        + lax.broadcasted_iota(jnp.int32, (hr, hc), 1) * 1274126177
    )
    seed_term = seed[0] * 374761393

    def hash_slot(source, pair, place):
        first = place * rows

        @pl.loop(0, rows // hr)
        def _(b):
            for side in range(2):
                j = (2 * source + core) * rows + b * hr
                x = base + (seed_term + j * 668265263 + side * HALF_STEP)
                x = x ^ lax.shift_right_logical(x, 15)
                x = x * 2146121005
                x = x ^ lax.shift_right_logical(x, 13)
                x = x * 1948299397
                code = (lax.shift_right_logical(x, 8) ^ lax.shift_right_logical(x, 24)) & 255
                row0 = pl.multiple_of(side * 2 * rows + first + b * hr, hr)
                sk[pair, pl.ds(row0, hr), :] = (code.astype(F32) - 127.5).astype(BF)

    steps = half
    hash_slot(chip, steps - 1, 1)
    acc[...] = jnp.zeros_like(acc)
    tacc[...] = jnp.zeros_like(tacc)
    for one in ins:
        one.wait()
    pl.semaphore_wait(barrier, chips)

    def copy(src, dst, send, recv_, to):
        return pltpu.make_async_remote_copy(
            src_ref=src, dst_ref=dst, send_sem=send, recv_sem=recv_,
            device_id=to, device_id_type=pl.DeviceIdType.MESH,
        )

    to_partner = {"blk": partner}
    cut = rows // 2

    def move(way, piece, t, last=False):
        first = isinstance(t, int) and t == 0
        src = own_slot if first else 2 * (t - 1) + way
        dst = 2 * t if last else 2 * t + way
        span = pl.ds(piece * cut, cut)
        return copy(
            gath.at[src, span], gath.at[dst, span],
            ring_send.at[way, piece, t], ring_recv.at[way, piece, t],
            device(chip_at(ring + 1 - 2 * way)),
        )

    ways = [(way, piece) for piece in range(2) for way in range(2)]
    for way, piece in ways:
        move(way, piece, 0).start()
    left_copies = [
        copy(lv, lvp, pair_send.at[0], pair_recv.at[0], to_partner),
        copy(ld, ldp, pair_send.at[1], pair_recv.at[1], to_partner),
        copy(lp, lpp, pair_send.at[2], pair_recv.at[2], to_partner),
    ]
    for one in left_copies:
        one.start()

    def pos_copy(o):
        return copy(gpos.at[chip], gpos.at[chip], pos_send.at[o], pos_recv.at[o],
                    device(lax.rem(chip + o, chips)))

    @pl.loop(1, chips)
    def _(o):
        pos_copy(o).start()

    lane = lax.broadcasted_iota(jnp.int32, (rows, TILE), 1)
    sub = lax.broadcasted_iota(jnp.int32, (rows, TILE), 0)
    low = lane < TILE // 2

    def left_side(side, v_ref, l_ref, p_ref):
        v = v_ref[...].astype(F32)
        l = -l_ref[...].astype(F32)
        vt = pltpu.roll(v, TILE // 2, 1)
        lt = pltpu.roll(l, TILE // 2, 1)
        for q, (a, b, keep) in enumerate(
            ((v, l, True), (vt, lt, True), (vt, lt, False), (v, l, False))
        ):
            for part, m in enumerate((a, b)):
                m = jnp.where(low, m, 0.0) if keep else jnp.where(low, 0.0, m)
                xs[side, q * rows:(q + 1) * rows, part * TILE:(part + 1) * TILE] = m.astype(BF)
        f = (2 * p_ref[...] - total).astype(F32) + 0.25
        column = jnp.sum(
            jnp.where(lane == sub, jnp.broadcast_to(f, (rows, TILE)), 0.0), axis=1, keepdims=True
        )
        fls[side] = jnp.broadcast_to(column, (rows, TILE))

    left_side(0, lv, ld, lp)
    for one in left_copies:
        one.wait()
    left_side(1, lvp, ldp, lpp)
    hash_slot(chip_at(ring - 1), 0, 0)
    hash_slot(chip_at(ring + 1), 0, 1)

    @pl.loop(1, chips)
    def _(o):
        pos_copy(o).wait()

    rb = 32

    def process(s, chip_a, chip_b):
        y = gath[pl.ds(2 * s, 2)].reshape(2 * rows, 2 * TILE)
        pos = jnp.concatenate([gpos[chip_a], gpos[chip_b]], axis=1)
        fr = (2 * pos + 1 - total).astype(F32) + 0.25
        fr = jnp.broadcast_to(fr, (rb, 2 * rows))
        for side in range(2):
            num[side] = lax.dot_general(
                xs[side], y, (((1,), (1,)), ((), ())), preferred_element_type=F32
            )
        for side in range(2):
            for b in range(rows // rb):
                r0 = b * rb
                fl1 = fls[side, r0:r0 + rb, :]
                fl = jnp.concatenate([fl1, fl1], axis=1)
                inv = 2.0 / ((fl - fr) * (fl + fr))
                al = fl * inv
                be = fr * inv
                ar = num[side, r0:r0 + rb, :]
                ai = num[side, rows + r0:rows + r0 + rb, :]
                br = num[side, 2 * rows + r0:2 * rows + r0 + rb, :]
                bi = num[side, 3 * rows + r0:3 * rows + r0 + rb, :]
                u0 = side * 2 * rows + r0
                w = 2 * rows
                wblk[u0:u0 + rb, :w] = (al * ai + be * br).astype(BF)
                wblk[u0:u0 + rb, w:] = (be * ar - al * bi).astype(BF)
                wblk[u0 + rows:u0 + rows + rb, :w] = (be * bi - al * ar).astype(BF)
                wblk[u0 + rows:u0 + rows + rb, w:] = (be * ai + al * br).astype(BF)
        acc[...] += jnp.dot(wblk[...], sk[s], preferred_element_type=F32)
        right = y[:, TILE:]
        for h in range(2):
            tacc[h] += lax.dot_general(
                right, sk[s, h * 2 * rows:(h + 1) * 2 * rows, :],
                (((0,), (0,)), ((), ())), preferred_element_type=F32,
            )

    @pl.loop(0, steps - 2)
    def _(t):
        for way, piece in ways:
            copy(gath.at[2 * t + way, pl.ds(piece * cut, cut)],
                 gath.at[2 * t + way, pl.ds(piece * cut, cut)],
                 ring_send.at[way, piece, t], ring_recv.at[way, piece, t],
                 device(chip_at(ring + 1 - 2 * way))).wait_recv()
            move(way, piece, t + 1).start()
        hash_slot(chip_at(ring - t - 2), t + 1, 0)
        hash_slot(chip_at(ring + t + 2), t + 1, 1)
        process(t, chip_at(ring - t - 1), chip_at(ring + t + 1))

    t = steps - 2
    for way, piece in ways:
        move(way, piece, t).wait_recv()
        if way == piece:
            move(way, piece, t + 1, True).start()
    hash_slot(chip_at(ring - t - 2), t + 1, 0)
    process(t, chip_at(ring - t - 1), chip_at(ring + t + 1))
    for way in range(2):
        move(way, way, t + 1, True).wait_recv()
    process(t + 1, chip_at(ring - t - 2), chip)

    tsend[...] = tacc[0, :TILE // 2] - tacc[1, TILE // 2:]
    tsums = copy(tsend, trecv, pair_send.at[4], pair_recv.at[4], to_partner)
    sums = copy(acc.at[pl.ds(2 * rows, 2 * rows)], recv, pair_send.at[3], pair_recv.at[3], to_partner)
    tsums.start()
    sums.start()
    tsums.wait_recv()
    t_all = (tsend[...] + trecv[...]) * (2.0 / (128.0 * total))
    t_high = t_all.astype(BF)
    t_low = (t_all - t_high.astype(F32)).astype(BF)
    t_stack = jnp.concatenate([t_high, t_high, t_low, t_low], axis=0)
    own_l = ld[...].astype(F32)
    hat1 = fls[0] * (1.0 / total)
    hat = jnp.concatenate([hat1] * (SKETCH // TILE), axis=1)
    l_re = jnp.where(low, own_l, 0.0).astype(BF)
    l_im = jnp.where(low, 0.0, own_l).astype(BF)
    extra_u = jnp.dot(jnp.concatenate([l_re, l_re], 1), t_stack, preferred_element_type=F32)
    extra_l = jnp.dot(jnp.concatenate([l_im, l_im], 1), t_stack, preferred_element_type=F32)
    sums.wait_recv()
    up = (acc[:rows] + recv[:rows]) * (1.0 / 128.0)
    lo = (acc[rows:2 * rows] + recv[rows:]) * (1.0 / 128.0)
    s_up = extra_u - hat * lo
    s_lo = extra_l + hat * up
    zs[0, :rows] = up.astype(BF)
    zs[0, rows:] = lo.astype(BF)
    zs[1, :rows] = s_up.astype(BF)
    zs[1, rows:] = s_lo.astype(BF)
    rows_copy = copy(zs.at[1 - core], zrecv, pair_send.at[5], pair_recv.at[5], to_partner)
    rows_copy.start()
    out[0] = up
    out[1] = lo
    out[2] = s_up
    out[3] = s_lo
    chunk = chunk_rows_of(chips)
    if chunk * chips > len(TILES) * TILE:
        pad = chunk * chips - len(TILES) * TILE
        gpart[len(TILES) * TILE:, :] = jnp.zeros((pad, TILE), BF)
    rows_copy.wait_recv()
    own = zs[core]
    other = zrecv[...]
    terms = []
    trace = jnp.zeros((1, 1), F32)
    for p in range(SKETCH // TILE):
        term = None
        for z in (own, other):
            d = lax.dot_general(
                z[:, p * TILE:(p + 1) * TILE], z[:, p * TILE:],
                (((0,), (0,)), ((), ())), preferred_element_type=F32,
            )
            term = d if term is None else term + d
        term = term * (1.0 / (2 * total))
        terms.append(term)
        diagonal = jnp.where(lane == sub, term[:, :TILE], 0.0)
        trace = trace + jnp.sum(jnp.sum(diagonal, axis=1, keepdims=True), axis=0, keepdims=True)
    mean = trace * (1.0 / SKETCH)
    mus[core, chip] = jnp.broadcast_to(mean, (1, TILE))
    at = 0
    for p in range(SKETCH // TILE):
        for q in range(SKETCH // TILE - p):
            tile = terms[p][:, q * TILE:(q + 1) * TILE]
            if q == 0:
                tile = jnp.where(lane == sub, tile - mean, tile)
            gpart[at * TILE:(at + 1) * TILE, :] = tile.astype(BF)
            at += 1

    def span_of(index):
        return pl.ds(pl.multiple_of(index * chunk, 16), chunk)

    def z_at(o):
        return lax.rem(row_z + o, half)

    neighbour = device(2 * row_z + 1 - row_y)

    def y_copy(o):
        return copy(gpart.at[span_of(2 * z_at(o) + 1 - row_y)], yrecv.at[o],
                    y_send.at[o], y_recv.at[o], neighbour)

    def z_copy(o):
        return copy(zsend.at[o], zgot.at[o], z_send.at[o], z_recv.at[o],
                    device(2 * z_at(o) + row_y))

    def mu_copy(o):
        return copy(mus.at[core, chip], mus.at[core, chip], mu_send.at[o], mu_recv.at[o],
                    device(lax.rem(chip + o, chips)))

    @pl.loop(1, half)
    def _(o):
        y_copy(o).start()

    y_copy(0).start()

    @pl.loop(1, chips)
    def _(o):
        mu_copy(o).start()

    @pl.loop(1, half)
    def _(o):
        y_copy(o).wait_recv()
        part = gpart[span_of(2 * z_at(o) + row_y), :].astype(F32) + yrecv[o].astype(F32)
        zsend[o] = part.astype(BF)
        z_copy(o).start()

    y_copy(0).wait_recv()
    share = gpart[span_of(chip), :].astype(F32) + yrecv[0].astype(F32)

    def add(o, value):
        z_copy(o).wait_recv()
        return value + zgot[o].astype(F32)

    share = lax.fori_loop(1, half, add, share)
    gall[core, span_of(chip), :] = share.astype(BF)

    def spread(o, column, send, recv_, to):
        place = span_of(2 * z_at(half - o) + column)
        return copy(gall.at[core, place], gall.at[core, place], send, recv_, to)

    def az_copy(o):
        place = span_of(chip)
        return copy(gall.at[core, place], gall.at[core, place], az_send.at[o], az_recv.at[o],
                    device(2 * z_at(o) + row_y))

    def ay_copy(o):
        return spread(o, row_y, ay_send.at[o], ay_recv.at[o], neighbour)

    def core_copy(o, other_column):
        column = 1 - row_y if other_column else row_y
        i = 1 if other_column else 0
        return spread(o, column, core_send.at[i, o], core_recv.at[i, o], to_partner)

    @pl.loop(1, half)
    def _(o):
        az_copy(o).start()

    ay_copy(0).start()
    core_copy(0, False).start()

    @pl.loop(1, chips)
    def _(o):
        mu_copy(o).wait_recv()

    mu_swap = copy(mus.at[core], mus.at[core], pair_send.at[6], pair_recv.at[6], to_partner)
    mu_swap.start()

    @pl.loop(1, half)
    def _(o):
        az_copy(o).wait_recv()
        ay_copy(o).start()
        core_copy(o, False).start()

    @pl.loop(0, half)
    def _(o):
        ay_copy(o).wait_recv()
        core_copy(o, True).start()

    @pl.loop(0, half)
    def _(o):
        core_copy(o, False).wait()
        core_copy(o, True).wait()
        ay_copy(o).wait_send()
        y_copy(o).wait_send()

    @pl.loop(1, half)
    def _(o):
        z_copy(o).wait_send()
        az_copy(o).wait_send()

    @pl.loop(1, chips)
    def _(o):
        mu_copy(o).wait_send()

    mu_swap.wait()
    for way, piece in ways:
        move(way, piece, 0).wait_send()

        @pl.loop(1, steps - 1)
        def _(t):
            move(way, piece, t).wait_send()

    for way in range(2):
        move(way, way, steps - 1, True).wait_send()
    sums.wait_send()
    tsums.wait_send()
    rows_copy.wait_send()


def finish(chips, sketches, gall, mus, out_l, out_s, gram_l, gram_s, full, sems):
    first = pltpu.make_async_copy(sketches.at[pl.ds(0, 2)], out_l, sems.at[0])
    second = pltpu.make_async_copy(sketches.at[pl.ds(2, 2)], out_s, sems.at[1])
    first.start()
    second.start()
    lane = lax.broadcasted_iota(jnp.int32, (TILE, TILE), 1)
    sub = lax.broadcasted_iota(jnp.int32, (TILE, TILE), 0)
    copies = []
    for which, out in enumerate((gram_l, gram_s)):
        mean = jnp.sum(mus[which], axis=0)
        for at, (p, q) in enumerate(TILES):
            tile = gall[which, at * TILE:(at + 1) * TILE, :].astype(F32)
            if q == p:
                tile = jnp.where(lane == sub, tile + mean, tile)
            else:
                full[which, q * TILE:(q + 1) * TILE, p * TILE:(p + 1) * TILE] = tile.T
            full[which, p * TILE:(p + 1) * TILE, q * TILE:(q + 1) * TILE] = tile
        one = pltpu.make_async_copy(full.at[which], out, sems.at[2 + which])
        one.start()
        copies.append(one)
    for one in [first, second] + copies:
        one.wait()


def solution(mesh):
    blk = mesh.shape["blk"]
    chips = blk // 2
    half = chips // 2

    def per_device(left_values, left_dirs, left_pos, right_dirs, right_values, right_pos, seed):
        rows = left_pos.shape[0]
        chunk = chunk_rows_of(chips)
        vmem = pl.BlockSpec(memory_space=pltpu.VMEM)
        hbm = pl.BlockSpec(memory_space=pltpu.HBM)
        dma = pltpu.SemaphoreType.DMA
        sketches, gall, mus = pl.pallas_call(
            functools.partial(kernel, blk),
            out_shape=(
                jax.ShapeDtypeStruct((4, rows, SKETCH), F32),
                jax.ShapeDtypeStruct((2, chunk * chips, TILE), BF),
                jax.ShapeDtypeStruct((2, chips, 1, TILE), F32),
            ),
            in_specs=[hbm] * 6 + [pl.BlockSpec(memory_space=pltpu.SMEM)],
            out_specs=(vmem,) * 3,
            scratch_shapes=[
                pltpu.VMEM((rows, TILE), BF),
                pltpu.VMEM((rows, TILE), BF),
                pltpu.VMEM((1, rows), jnp.int32),
                pltpu.VMEM((rows, TILE), BF),
                pltpu.VMEM((rows, TILE), BF),
                pltpu.VMEM((1, rows), jnp.int32),
                pltpu.VMEM((chips, rows, 2 * TILE), BF),
                pltpu.VMEM((chips, 1, rows), jnp.int32),
                pltpu.VMEM((2, 4 * rows, 2 * TILE), BF),
                pltpu.VMEM((2, rows, TILE), F32),
                pltpu.VMEM((2, 4 * rows, 2 * rows), F32),
                pltpu.VMEM((4 * rows, 4 * rows), BF),
                pltpu.VMEM((chips // 2, 4 * rows, SKETCH), BF),
                pltpu.VMEM((4 * rows, SKETCH), F32),
                pltpu.VMEM((2, TILE, SKETCH), F32),
                pltpu.VMEM((2 * rows, SKETCH), F32),
                pltpu.VMEM((TILE // 2, SKETCH), F32),
                pltpu.VMEM((TILE // 2, SKETCH), F32),
                pltpu.VMEM((2, 2 * rows, SKETCH), BF),
                pltpu.VMEM((2 * rows, SKETCH), BF),
                pltpu.VMEM((chunk * chips, TILE), BF),
                pltpu.VMEM((half, chunk, TILE), BF),
                pltpu.VMEM((half, chunk, TILE), BF),
                pltpu.VMEM((half, chunk, TILE), BF),
                dma((6,)), dma((8,)), dma((8,)),
                dma((2, 2, half)), dma((2, 2, half)),
                dma((chips,)), dma((chips,)),
                dma((half,)), dma((half,)), dma((half,)), dma((half,)),
                dma((half,)), dma((half,)), dma((half,)), dma((half,)),
                dma((2, half)), dma((2, half)),
                dma((chips,)), dma((chips,)),
            ],
            compiler_params=pltpu.CompilerParams(
                collective_id=0, has_side_effects=True, vmem_limit_bytes=48 * 1024 * 1024
            ),
        )(
            left_values, left_dirs, left_pos.reshape(1, rows),
            right_dirs, right_values, right_pos.reshape(1, rows), seed,
        )
        return pl.pallas_call(
            functools.partial(finish, chips),
            out_shape=(
                jax.ShapeDtypeStruct((2, rows, SKETCH), F32),
                jax.ShapeDtypeStruct((2, rows, SKETCH), F32),
                jax.ShapeDtypeStruct((SKETCH, SKETCH), F32),
                jax.ShapeDtypeStruct((SKETCH, SKETCH), F32),
            ),
            in_specs=[vmem] * 3,
            out_specs=(hbm,) * 4,
            scratch_shapes=[pltpu.VMEM((2, SKETCH, SKETCH), F32), dma((4,))],
            compiler_params=pltpu.CompilerParams(vmem_limit_bytes=32 * 1024 * 1024),
        )(sketches, gall, mus)

    return jax.shard_map(
        per_device,
        mesh=mesh,
        in_specs=(
            P(("grp", "blk"), None),
            P(("grp", "blk"), None),
            P(("grp", "blk")),
            P(("grp", "blk"), None),
            P(("grp", "blk"), None),
            P(("grp", "blk")),
            P("grp"),
        ),
        out_specs=(P("grp", "blk", None), P("grp", "blk", None), P("grp", None), P("grp", None)),
        check_vma=False,
    )
```

time: 212 us -> 51.3 us (0.24)
  waiting for transfers between devices: 94.3 us -> 0 us
  blocking collectives: 62.6 us -> 0 us
  Pallas kernels: 0 us -> 45.9 us
  matrix products: 20.7 us -> 0 us
  other arithmetic: 17 us -> 0 us
  between operations: 14.7 us -> 1.31 us
  local copies, waits for them, and re-layouts: 1.46 us -> 3.69 us
    psum x1 -> x0, waiting for transfers between devices: 94.3 us -> none  [per_device(): lax.psum((gram_term(halves[0]), gram_term(halves[1])), 'blk')]
    all_gather x3 -> x0, blocking collectives: 62.6 us -> none  [the longest x1 24.8 us: per_device(): piece_dirs = lax.all_gather(right_dirs, 'blk', axis=0, tiled=True)]
    pallas_call x0 -> x2, Pallas kernels: none -> 45.9 us  [the longest x1 44.2 us: per_device(): pl.pallas_call(functools.partial(kernel, blk), out_shape=(jax.ShapeDtypeS...]
    dot_general x14 -> x0, matrix products: 20.7 us -> none  [the longest x4 7.89 us: pencil_blocks(): return jnp.dot(blocks, stacked_sketch, preferred_element_type=jnp.float32)]
    another operation x12 -> x0, other arithmetic: 8.69 us -> none
    convert_element_type x4 -> x0, other arithmetic: 4.2 us -> none  [sketch_block(): ((level_code.astype(jnp.float32) - 127.5) / 128.0).astype(jnp.bfloat16)]
    unnamed x4 -> x12, local copies, waits for them, and re-layouts: 0.01 us -> 3.69 us
    div x6 -> x0, other arithmetic: 3.43 us -> none  [the longest x1 3.09 us: per_device(): gram_shifted / (2 * total_left)]
  transfers between devices with their start and end apart: 1 -> 0, of which waited for: 1 -> 0; matrix products, arithmetic and copies ran while one was open for 0% -> 0% of each run, Pallas kernels for 0% -> 0%
where the time goes in v1:
time: 51.3 us; the launch traced here: 50.8 us
  Pallas kernels  45.9 us (89%)
  local copies, waits for them, and re-layouts  3.69 us (7%)
  between operations  1.31 us (3%)
    pallas_call x1, Pallas kernels, per_device(): pl.pallas_call(functools.partial(kernel, blk), out_shape=(jax.ShapeDtypeS...  44.2 us
    unnamed x12, local copies, waits for them, and re-layouts  3.69 us
    pallas_call x1, Pallas kernels, per_device(): pl.pallas_call(functools.partial(finish, chips), out_shape=(jax.ShapeDtyp...  1.7 us

profile of v1, /device:TPU:0, one launch (start us, length us, event | category | flops | bytes accessed | tf_op | source)
XLA Modules:
  0.0 50.8 jit_solution(18250375135226766321)
XLA Ops:
  1.3 0.0 copy-start.4
  1.3 0.0 copy-start.5
  1.3 0.6 %copy-done.4 = s32[128]{0:T(128)S(1)} copy-done((s32[128]{0:T(128)S(1)}, s32[128]{0:T(128)}, u32[]{:S(2)}) %copy-start.4) | copy-done | bytes 536
  1.9 0.0 copy-done.5
  2.0 0.0 copy-start
  2.0 0.8 %copy-done = bf16[128,128]{1,0:T(8,128)(2,1)S(1)} copy-done((bf16[128,128]{1,0:T(8,128)(2,1)S(1)}, bf16[128,128]{1,0:T(8,128)(2,1)}, u32[]{:S(2)}) %copy-start) | copy-done | bytes 32792
  2.7 0.0 copy-start.1
  2.7 0.8 %copy-done.1 = bf16[128,128]{1,0:T(8,128)(2,1)S(1)} copy-done((bf16[128,128]{1,0:T(8,128)(2,1)S(1)}, bf16[128,128]{1,0:T(8,128)(2,1)}, u32[]{:S(2)}) %copy-start.1) | copy-done | bytes 32792
  3.5 0.0 copy-start.2
  3.5 0.8 %copy-done.2 = bf16[128,128]{1,0:T(8,128)(2,1)S(1)} copy-done((bf16[128,128]{1,0:T(8,128)(2,1)S(1)}, bf16[128,128]{1,0:T(8,128)(2,1)}, u32[]{:S(2)}) %copy-start.2) | copy-done | bytes 32792
  4.2 0.0 copy-start.3
  4.2 0.8 %copy-done.3 = bf16[128,128]{1,0:T(8,128)(2,1)S(1)} copy-done((bf16[128,128]{1,0:T(8,128)(2,1)S(1)}, bf16[128,128]{1,0:T(8,128)(2,1)}, u32[]{:S(2)}) %copy-start.3) | copy-done | bytes 32792
  5.0 44.2 %shard_map.102 = (f32[4,128,512]{2,1,0:T(8,128)S(1)}, bf16[2,1280,128]{2,1,0:T(8,128)(2,1)S(1)}, f32[2,8,1,128]{3,2,1,0:T(1,128)S(1)}) custom-call(bf16[128,128]{1,0:T(8,128)(2,1)S(1)} %copy-done, bf16[128,128]{1,0:T(8,128)(2,1)S(1)} %copy-done.1, s32[1,128]{1,0:T(1,128)S(1)} %bitcast.2, bf16[128,128]{1,0:T(8,128)(2,1)S(1)} %copy-done.2, ...), custom_call_target="tpu_custom_call" | custom-call | tf_op jit(solution)/shard_map/pallas_call | solution.py:464
  49.1 1.7 %shard_map.103 = (f32[2,128,512]{2,1,0:T(8,128)}, f32[2,128,512]{2,1,0:T(8,128)}, f32[512,512]{1,0:T(8,128)}, f32[512,512]{1,0:T(8,128)}) custom-call(f32[4,128,512]{2,1,0:T(8,128)S(1)} %get-tuple-element.7.sketches, bf16[2,1280,128]{2,1,0:T(8,128)(2,1)S(1)} %get-tuple-element.8.gall, f32[2,8,1,128]{3,2,1,0:T(1,128)S(1)} %get-tuple-element.9.mus), custom_call_target="tpu_custom_call" | custom-call | tf_op jit(solution)/shard_map/pallas_call | solution.py:513
Async XLA Ops:
  1.3 0.7 %copy-start.4 = (s32[128]{0:T(128)S(1)}, s32[128]{0:T(128)}, u32[]{:S(2)}) copy-start(s32[128]{0:T(128)} %param.9) | copy-start | bytes 1540
  1.3 0.7 %copy-start.5 = (s32[128]{0:T(128)S(1)}, s32[128]{0:T(128)}, u32[]{:S(2)}) copy-start(s32[128]{0:T(128)} %param.12) | copy-start | bytes 1540
  2.0 0.8 %copy-start = (bf16[128,128]{1,0:T(8,128)(2,1)S(1)}, bf16[128,128]{1,0:T(8,128)(2,1)}, u32[]{:S(2)}) copy-start(bf16[128,128]{1,0:T(8,128)(2,1)} %lv_in.1) | copy-start | bytes 98308
  2.7 0.8 %copy-start.1 = (bf16[128,128]{1,0:T(8,128)(2,1)S(1)}, bf16[128,128]{1,0:T(8,128)(2,1)}, u32[]{:S(2)}) copy-start(bf16[128,128]{1,0:T(8,128)(2,1)} %ld_in.1) | copy-start | bytes 98308
  3.5 0.8 %copy-start.2 = (bf16[128,128]{1,0:T(8,128)(2,1)S(1)}, bf16[128,128]{1,0:T(8,128)(2,1)}, u32[]{:S(2)}) copy-start(bf16[128,128]{1,0:T(8,128)(2,1)} %rd_in.1) | copy-start | bytes 98308
  4.2 0.8 %copy-start.3 = (bf16[128,128]{1,0:T(8,128)(2,1)S(1)}, bf16[128,128]{1,0:T(8,128)(2,1)}, u32[]{:S(2)}) copy-start(bf16[128,128]{1,0:T(8,128)(2,1)} %rw_in.1) | copy-start | bytes 98308

commit v2 on v1

--- a/solution.py
+++ b/solution.py
@@ -47,15 +47,13 @@
 
     row_y = lax.rem(chip, 2)
     row_z = chip // 2
-    ring = (1 - 2 * row_y) * row_z + row_y * (2 * half - 1)
-
-    def chip_at(position):
-        q = lax.rem(position + 2 * chips, chips)
-        y = q // half
-        z = (1 - y) * q + y * (2 * half - 1 - q)
-        return 2 * z + y
-
-    own_slot = chips - 1
+
+    def z_at(o):
+        return lax.rem(row_z + o, half)
+
+    neighbour = device(2 * row_z + 1 - row_y)
+
+    own_slot = 0
     ins = [
         pltpu.make_async_copy(src, dst, in_sem.at[i])
         for i, (src, dst) in enumerate((
@@ -73,10 +71,12 @@
         barrier, inc=1, device_id={"blk": partner}, device_id_type=pl.DeviceIdType.MESH
     )
 
-    @pl.loop(1, chips)
+    pl.semaphore_signal(barrier, inc=1, device_id=neighbour, device_id_type=pl.DeviceIdType.MESH)
+
+    @pl.loop(1, half)
     def _(o):
         pl.semaphore_signal(
-            barrier, inc=1, device_id=device(lax.rem(chip + o, chips)),
+            barrier, inc=1, device_id=device(2 * z_at(o) + row_y),
             device_id_type=pl.DeviceIdType.MESH,
         )
 
@@ -103,13 +103,12 @@
                 row0 = pl.multiple_of(side * 2 * rows + first + b * hr, hr)
                 sk[pair, pl.ds(row0, hr), :] = (code.astype(F32) - 127.5).astype(BF)
 
-    steps = half
-    hash_slot(chip, steps - 1, 1)
+    hash_slot(chip, 0, 0)
     acc[...] = jnp.zeros_like(acc)
     tacc[...] = jnp.zeros_like(tacc)
     for one in ins:
         one.wait()
-    pl.semaphore_wait(barrier, chips)
+    pl.semaphore_wait(barrier, half + 1)
 
     def copy(src, dst, send, recv_, to):
         return pltpu.make_async_remote_copy(
@@ -118,22 +117,35 @@
         )
 
     to_partner = {"blk": partner}
-    cut = rows // 2
-
-    def move(way, piece, t, last=False):
-        first = isinstance(t, int) and t == 0
-        src = own_slot if first else 2 * (t - 1) + way
-        dst = 2 * t if last else 2 * t + way
-        span = pl.ds(piece * cut, cut)
-        return copy(
-            gath.at[src, span], gath.at[dst, span],
-            ring_send.at[way, piece, t], ring_recv.at[way, piece, t],
-            device(chip_at(ring + 1 - 2 * way)),
-        )
-
-    ways = [(way, piece) for piece in range(2) for way in range(2)]
-    for way, piece in ways:
-        move(way, piece, 0).start()
+
+    def origin(o, column):
+        return 2 * z_at(half - o) + column
+
+    def along_z(o):
+        return copy(gath.at[0], gath.at[2 * o], ring_send.at[0, o], ring_recv.at[0, o],
+                    device(2 * z_at(o) + row_y))
+
+    def along_y(o):
+        return copy(gath.at[2 * o], gath.at[2 * o + 1], ring_send.at[1, o], ring_recv.at[1, o],
+                    neighbour)
+
+    def pos_z(o):
+        return copy(gpos.at[chip], gpos.at[chip], pos_send.at[0, o], pos_recv.at[0, o],
+                    device(2 * z_at(o) + row_y))
+
+    def pos_y(o):
+        place = origin(o, row_y)
+        return copy(gpos.at[place], gpos.at[place], pos_send.at[1, o], pos_recv.at[1, o],
+                    neighbour)
+
+    along_y(0).start()
+    pos_y(0).start()
+
+    @pl.loop(1, half)
+    def _(o):
+        along_z(o).start()
+        pos_z(o).start()
+
     left_copies = [
         copy(lv, lvp, pair_send.at[0], pair_recv.at[0], to_partner),
         copy(ld, ldp, pair_send.at[1], pair_recv.at[1], to_partner),
@@ -141,14 +153,6 @@
     ]
     for one in left_copies:
         one.start()
-
-    def pos_copy(o):
-        return copy(gpos.at[chip], gpos.at[chip], pos_send.at[o], pos_recv.at[o],
-                    device(lax.rem(chip + o, chips)))
-
-    @pl.loop(1, chips)
-    def _(o):
-        pos_copy(o).start()
 
     lane = lax.broadcasted_iota(jnp.int32, (rows, TILE), 1)
     sub = lax.broadcasted_iota(jnp.int32, (rows, TILE), 0)
@@ -175,12 +179,7 @@
     for one in left_copies:
         one.wait()
     left_side(1, lvp, ldp, lpp)
-    hash_slot(chip_at(ring - 1), 0, 0)
-    hash_slot(chip_at(ring + 1), 0, 1)
-
-    @pl.loop(1, chips)
-    def _(o):
-        pos_copy(o).wait()
+    hash_slot(origin(0, 1 - row_y), 0, 1)
 
     rb = 32
 
@@ -219,28 +218,24 @@
                 (((0,), (0,)), ((), ())), preferred_element_type=F32,
             )
 
-    @pl.loop(0, steps - 2)
-    def _(t):
-        for way, piece in ways:
-            copy(gath.at[2 * t + way, pl.ds(piece * cut, cut)],
-                 gath.at[2 * t + way, pl.ds(piece * cut, cut)],
-                 ring_send.at[way, piece, t], ring_recv.at[way, piece, t],
-                 device(chip_at(ring + 1 - 2 * way))).wait_recv()
-            move(way, piece, t + 1).start()
-        hash_slot(chip_at(ring - t - 2), t + 1, 0)
-        hash_slot(chip_at(ring + t + 2), t + 1, 1)
-        process(t, chip_at(ring - t - 1), chip_at(ring + t + 1))
-
-    t = steps - 2
-    for way, piece in ways:
-        move(way, piece, t).wait_recv()
-        if way == piece:
-            move(way, piece, t + 1, True).start()
-    hash_slot(chip_at(ring - t - 2), t + 1, 0)
-    process(t, chip_at(ring - t - 1), chip_at(ring + t + 1))
-    for way in range(2):
-        move(way, way, t + 1, True).wait_recv()
-    process(t + 1, chip_at(ring - t - 2), chip)
+    along_y(0).wait_recv()
+    pos_y(0).wait_recv()
+    process(0, chip, origin(0, 1 - row_y))
+
+    @pl.loop(1, half)
+    def _(o):
+        hash_slot(origin(o, row_y), o, 0)
+        hash_slot(origin(o, 1 - row_y), o, 1)
+        along_z(o).wait_recv()
+        along_y(o).start()
+        pos_z(o).wait_recv()
+        pos_y(o).start()
+
+    @pl.loop(1, half)
+    def _(o):
+        along_y(o).wait_recv()
+        pos_y(o).wait_recv()
+        process(o, origin(o, row_y), origin(o, 1 - row_y))
 
     tsend[...] = tacc[0, :TILE // 2] - tacc[1, TILE // 2:]
     tsums = copy(tsend, trecv, pair_send.at[4], pair_recv.at[4], to_partner)
@@ -309,11 +304,6 @@
     def span_of(index):
         return pl.ds(pl.multiple_of(index * chunk, 16), chunk)
 
-    def z_at(o):
-        return lax.rem(row_z + o, half)
-
-    neighbour = device(2 * row_z + 1 - row_y)
-
     def y_copy(o):
         return copy(gpart.at[span_of(2 * z_at(o) + 1 - row_y)], yrecv.at[o],
                     y_send.at[o], y_recv.at[o], neighbour)
@@ -322,9 +312,14 @@
         return copy(zsend.at[o], zgot.at[o], z_send.at[o], z_recv.at[o],
                     device(2 * z_at(o) + row_y))
 
-    def mu_copy(o):
-        return copy(mus.at[core, chip], mus.at[core, chip], mu_send.at[o], mu_recv.at[o],
-                    device(lax.rem(chip + o, chips)))
+    def mu_z(o):
+        return copy(mus.at[core, chip], mus.at[core, chip], mu_send.at[0, o], mu_recv.at[0, o],
+                    device(2 * z_at(o) + row_y))
+
+    def mu_y(o):
+        place = origin(o, row_y)
+        return copy(mus.at[core, place], mus.at[core, place], mu_send.at[1, o], mu_recv.at[1, o],
+                    neighbour)
 
     @pl.loop(1, half)
     def _(o):
@@ -332,9 +327,11 @@
 
     y_copy(0).start()
 
-    @pl.loop(1, chips)
-    def _(o):
-        mu_copy(o).start()
+    mu_y(0).start()
+
+    @pl.loop(1, half)
+    def _(o):
+        mu_z(o).start()
 
     @pl.loop(1, half)
     def _(o):
@@ -377,9 +374,14 @@
     ay_copy(0).start()
     core_copy(0, False).start()
 
-    @pl.loop(1, chips)
-    def _(o):
-        mu_copy(o).wait_recv()
+    @pl.loop(1, half)
+    def _(o):
+        mu_z(o).wait_recv()
+        mu_y(o).start()
+
+    @pl.loop(0, half)
+    def _(o):
+        mu_y(o).wait_recv()
 
     mu_swap = copy(mus.at[core], mus.at[core], pair_send.at[6], pair_recv.at[6], to_partner)
     mu_swap.start()
@@ -407,20 +409,19 @@
         z_copy(o).wait_send()
         az_copy(o).wait_send()
 
-    @pl.loop(1, chips)
-    def _(o):
-        mu_copy(o).wait_send()
+    @pl.loop(1, half)
+    def _(o):
+        mu_z(o).wait_send()
+        along_z(o).wait_send()
+        pos_z(o).wait_send()
+
+    @pl.loop(0, half)
+    def _(o):
+        mu_y(o).wait_send()
+        along_y(o).wait_send()
+        pos_y(o).wait_send()
 
     mu_swap.wait()
-    for way, piece in ways:
-        move(way, piece, 0).wait_send()
-
-        @pl.loop(1, steps - 1)
-        def _(t):
-            move(way, piece, t).wait_send()
-
-    for way in range(2):
-        move(way, way, steps - 1, True).wait_send()
     sums.wait_send()
     tsums.wait_send()
     rows_copy.wait_send()
@@ -496,12 +497,12 @@
                 pltpu.VMEM((half, chunk, TILE), BF),
                 pltpu.VMEM((half, chunk, TILE), BF),
                 dma((6,)), dma((8,)), dma((8,)),
-                dma((2, 2, half)), dma((2, 2, half)),
-                dma((chips,)), dma((chips,)),
+                dma((2, half)), dma((2, half)),
+                dma((2, half)), dma((2, half)),
                 dma((half,)), dma((half,)), dma((half,)), dma((half,)),
                 dma((half,)), dma((half,)), dma((half,)), dma((half,)),
                 dma((2, half)), dma((2, half)),
-                dma((chips,)), dma((chips,)),
+                dma((2, half)), dma((2, half)),
             ],
             compiler_params=pltpu.CompilerParams(
                 collective_id=0, has_side_effects=True, vmem_limit_bytes=48 * 1024 * 1024

time: 51.3 us -> 46.1 us (0.90)
  Pallas kernels: 45.9 us -> 40.7 us
    pallas_call x1, Pallas kernels: 44.2 us -> 39 us  [per_device(): pl.pallas_call(functools.partial(kernel, blk), out_shape=(jax.ShapeDtypeS...]
where the time goes in v2:
time: 46.1 us; the launch traced here: 45.7 us
  Pallas kernels  40.7 us (88%)
  local copies, waits for them, and re-layouts  3.69 us (8%)
  between operations  1.31 us (3%)
    pallas_call x1, Pallas kernels, per_device(): pl.pallas_call(functools.partial(kernel, blk), out_shape=(jax.ShapeDtypeS...  39 us
    unnamed x12, local copies, waits for them, and re-layouts  3.69 us
    pallas_call x1, Pallas kernels, per_device(): pl.pallas_call(functools.partial(finish, chips), out_shape=(jax.ShapeDtyp...  1.7 us

profile of v2, /device:TPU:0, one launch (start us, length us, event | category | flops | bytes accessed | tf_op | source)
XLA Modules:
  0.0 45.7 jit_solution(1458511632022887680)
XLA Ops:
  1.3 0.0 copy-start.4
  1.3 0.0 copy-start.5
  1.3 0.6 %copy-done.4 = s32[128]{0:T(128)S(1)} copy-done((s32[128]{0:T(128)S(1)}, s32[128]{0:T(128)}, u32[]{:S(2)}) %copy-start.4) | copy-done | bytes 536
  1.9 0.0 copy-done.5
  2.0 0.0 copy-start
  2.0 0.8 %copy-done = bf16[128,128]{1,0:T(8,128)(2,1)S(1)} copy-done((bf16[128,128]{1,0:T(8,128)(2,1)S(1)}, bf16[128,128]{1,0:T(8,128)(2,1)}, u32[]{:S(2)}) %copy-start) | copy-done | bytes 32792
  2.7 0.0 copy-start.1
  2.7 0.8 %copy-done.1 = bf16[128,128]{1,0:T(8,128)(2,1)S(1)} copy-done((bf16[128,128]{1,0:T(8,128)(2,1)S(1)}, bf16[128,128]{1,0:T(8,128)(2,1)}, u32[]{:S(2)}) %copy-start.1) | copy-done | bytes 32792
  3.5 0.0 copy-start.2
  3.5 0.8 %copy-done.2 = bf16[128,128]{1,0:T(8,128)(2,1)S(1)} copy-done((bf16[128,128]{1,0:T(8,128)(2,1)S(1)}, bf16[128,128]{1,0:T(8,128)(2,1)}, u32[]{:S(2)}) %copy-start.2) | copy-done | bytes 32792
  4.2 0.0 copy-start.3
  4.2 0.8 %copy-done.3 = bf16[128,128]{1,0:T(8,128)(2,1)S(1)} copy-done((bf16[128,128]{1,0:T(8,128)(2,1)S(1)}, bf16[128,128]{1,0:T(8,128)(2,1)}, u32[]{:S(2)}) %copy-start.3) | copy-done | bytes 32792
  5.0 39.0 %shard_map.102 = (f32[4,128,512]{2,1,0:T(8,128)S(1)}, bf16[2,1280,128]{2,1,0:T(8,128)(2,1)S(1)}, f32[2,8,1,128]{3,2,1,0:T(1,128)S(1)}) custom-call(bf16[128,128]{1,0:T(8,128)(2,1)S(1)} %copy-done, bf16[128,128]{1,0:T(8,128)(2,1)S(1)} %copy-done.1, s32[1,128]{1,0:T(1,128)S(1)} %bitcast.2, bf16[128,128]{1,0:T(8,128)(2,1)S(1)} %copy-done.2, ...), custom_call_target="tpu_custom_call" | custom-call | tf_op jit(solution)/shard_map/pallas_call | solution.py:465
  44.0 1.7 %shard_map.103 = (f32[2,128,512]{2,1,0:T(8,128)}, f32[2,128,512]{2,1,0:T(8,128)}, f32[512,512]{1,0:T(8,128)}, f32[512,512]{1,0:T(8,128)}) custom-call(f32[4,128,512]{2,1,0:T(8,128)S(1)} %get-tuple-element.7.sketches, bf16[2,1280,128]{2,1,0:T(8,128)(2,1)S(1)} %get-tuple-element.8.gall, f32[2,8,1,128]{3,2,1,0:T(1,128)S(1)} %get-tuple-element.9.mus), custom_call_target="tpu_custom_call" | custom-call | tf_op jit(solution)/shard_map/pallas_call | solution.py:514
Async XLA Ops:
  1.3 0.7 %copy-start.4 = (s32[128]{0:T(128)S(1)}, s32[128]{0:T(128)}, u32[]{:S(2)}) copy-start(s32[128]{0:T(128)} %param.9) | copy-start | bytes 1540
  1.3 0.7 %copy-start.5 = (s32[128]{0:T(128)S(1)}, s32[128]{0:T(128)}, u32[]{:S(2)}) copy-start(s32[128]{0:T(128)} %param.12) | copy-start | bytes 1540
  2.0 0.8 %copy-start = (bf16[128,128]{1,0:T(8,128)(2,1)S(1)}, bf16[128,128]{1,0:T(8,128)(2,1)}, u32[]{:S(2)}) copy-start(bf16[128,128]{1,0:T(8,128)(2,1)} %lv_in.1) | copy-start | bytes 98308
  2.7 0.8 %copy-start.1 = (bf16[128,128]{1,0:T(8,128)(2,1)S(1)}, bf16[128,128]{1,0:T(8,128)(2,1)}, u32[]{:S(2)}) copy-start(bf16[128,128]{1,0:T(8,128)(2,1)} %ld_in.1) | copy-start | bytes 98308
  3.5 0.8 %copy-start.2 = (bf16[128,128]{1,0:T(8,128)(2,1)S(1)}, bf16[128,128]{1,0:T(8,128)(2,1)}, u32[]{:S(2)}) copy-start(bf16[128,128]{1,0:T(8,128)(2,1)} %rd_in.1) | copy-start | bytes 98308
  4.2 0.8 %copy-start.3 = (bf16[128,128]{1,0:T(8,128)(2,1)S(1)}, bf16[128,128]{1,0:T(8,128)(2,1)}, u32[]{:S(2)}) copy-start(bf16[128,128]{1,0:T(8,128)(2,1)} %rw_in.1) | copy-start | bytes 98308
